TPU v7x, 256 devices: a whole 4x4x8 slice. The times are simulated.
256 devices in a mesh: gx: 32 (over y, z), gy: 4 (over x_lo, core), ma: 2 (over x_hi).
Axes of the slice: x: 4 (x_hi: 2, x_lo: 2; x = x_hi * 2 + x_lo), y: 4, z: 8, core: 2. Of those that a mesh axis runs over, the one named last changes fastest.
Arguments:
- x_modes: bfloat16 [64, 48, 128, 256], P('gx', 'gy', None, 'ma'), may hold values from -45 to 45
- p_dirs: bfloat16 [64, 48, 128, 256], P('gx', 'gy', None, 'ma'), may hold values from -45 to 45
- permittivity: float32 [64, 48, 128], P('gx', 'gy'), may hold values from 1 to 12
- ritz_values: float32 [256], P('ma'), may hold values from 0.05 to 1
- blocks: bfloat16 [16, 128, 128], replicated, may hold values from -0.25 to 0.25
- adj_types: int32 [5, 64, 48], P(None, 'gx', 'gy'), may hold values from 0 to 15
- x_link: int32 [2, 32, 48], P(None, 'gx', 'gy'), may hold values from 0 to 11
- coeffs: bfloat16 [3, 256, 256], replicated, may hold values from -0.21875 to 0.21875
Outputs:
- x_next: bfloat16 [64, 48, 128, 256], P('gx', 'gy', None, 'ma')
- gram_k: float32 [3, 256, 3, 256], P(None, None, None, 'ma')
- gram_m: float32 [3, 256, 3, 256], P(None, None, None, 'ma')
Inputs may be any that keep to these rules, and one draw needn't show every extreme that they name: `x_link`: a row counted within its group of 12 rows.
All inputs are finite; a program needn't handle non-finite values.
Results may differ from a plain program's by a relative error of at most 0.0075.
Values may be sent and summed in bfloat16 or wider, within the bound.
A program may use at most 128 MiB of HBM per device.

v0:
```python
import functools
import jax
import jax.numpy as jnp
from jax import lax
from jax.experimental import pallas as pl
from jax.experimental.pallas import tpu as pltpu
from jax.sharding import PartitionSpec as P

MESH = pl.DeviceIdType.MESH
F32 = jnp.float32
BF16 = jnp.bfloat16
EDGE = 128
HALF = 128
COLS = 2
ROWS = 12
PATCHES = COLS * ROWS
NZ = 8
NB = 8
KX, MX, MW, MP, KW, KP = range(6)
ROW_OF = ((0, 0), (1, 0), (2, 0), (0, 1), (2, 1), (1, 1))
GROUPS = (((0, 1, 2), (KX, MX, MW, MP)), ((0, 1, 2), (KW, KP)), ((3, 4, 5), (KX, MX, MW, MP, KW, KP)))
SIZES = tuple(len(r) * len(c) for r, c in GROUPS)
STARTS = tuple(sum(SIZES[:g]) for g in range(len(SIZES)))
TILES = sum(SIZES)
NORM_TILE = 1 * 4 + MW


def step_kernel(
    edges_total,
    x_hbm, p_hbm, perm_ref, ritz_ref, blocks_ref, adj_ref, link_ref, coef_ref,
    next_ref, gk_ref, gm_ref,
    fx, fp, fw, fa, xlo, xhi, plo, phi, wlo, whi, alo, ahi, p_far, w_far,
    eps, images, part, core_buf, z_out, z_buf, b_src, b_buf, total_buf, coef_own, scale_out, scale_in, ritz_out, ritz_in,
    load_sem, halo_send, halo_recv, far_send, far_recv,
    core_send, core_recv, z_send, z_recv, b_send, b_recv,
    back_send, back_recv, pair_send, pair_recv, scale_send, scale_recv, ritz_send, ritz_recv,
):
    gx, gy, ma = (lax.axis_index(a) for a in ("gx", "gy", "ma"))
    ngx, ngy = lax.axis_size("gx"), lax.axis_size("gy")
    z_id, y_id = lax.rem(gx, NZ), gx // NZ
    core, x_lo = lax.rem(gy, 2), gy // 2
    b_id = y_id * 2 + x_lo
    east, west = {"gx": lax.rem(gx + 1, ngx)}, {"gx": lax.rem(gx + ngx - 1, ngx)}
    north, south = {"gy": lax.rem(gy + 1, ngy)}, {"gy": lax.rem(gy + ngy - 1, ngy)}
    far, pair = {"ma": 1 - ma}, {"gy": gy + 1 - 2 * core}

    def z_peer(step):
        z_to = lax.rem(z_id + step, NZ)
        return z_to, {"gx": y_id * NZ + z_to}

    def b_peer(step):
        b_to = lax.rem(b_id + step, NB)
        return {"gx": (b_to // 2) * NZ + z_id, "gy": lax.rem(b_to, 2) * 2 + core}

    def remote(src, dst, send, recv, device):
        return pltpu.make_async_remote_copy(
            src_ref=src, dst_ref=dst, send_sem=send, recv_sem=recv, device_id=device, device_id_type=MESH
        )

    def start(copies):
        for copy in copies:
            copy.start()

    def wait(copies):
        for copy in copies:
            copy.wait()

    loads = [
        pltpu.make_async_copy(x_hbm, fx.at[:, pl.ds(1, ROWS)], load_sem.at[0]),
        pltpu.make_async_copy(p_hbm, fp.at[:, pl.ds(1, ROWS)], load_sem.at[1]),
    ]
    start(loads)

    barrier = pltpu.get_barrier_semaphore()
    for device in (east, west, north, south, far, pair):
        pl.semaphore_signal(barrier, inc=1, device_id=device, device_id_type=MESH)

    @pl.loop(1, NZ)
    def _(step):
        pl.semaphore_signal(barrier, inc=1, device_id=z_peer(step)[1], device_id_type=MESH)

    @pl.loop(1, NB)
    def _(step):
        pl.semaphore_signal(barrier, inc=1, device_id=b_peer(step), device_id_type=MESH)

    for col in range(COLS):
        @pl.loop(0, ROWS, unroll=4)
        def _(row):
            eps[col * ROWS + row] = jnp.broadcast_to(perm_ref[row, pl.ds(col, 1)], (EDGE, EDGE)).T

    ritz_out[...] = jnp.broadcast_to(ritz_ref[...], (8, HALF))
    ritz_copy = remote(ritz_out, ritz_in, ritz_send, ritz_recv, far)
    wait(loads)
    pl.semaphore_wait(barrier, 6 + NZ - 1 + NB - 1)

    def halo(k, field, low, high):
        return [
            remote(field.at[0, pl.ds(1, ROWS)], high, halo_send.at[k, 0], halo_recv.at[k, 0], west),
            remote(field.at[1, pl.ds(1, ROWS)], low, halo_send.at[k, 1], halo_recv.at[k, 1], east),
            remote(field.at[:, ROWS], field.at[:, 0], halo_send.at[k, 2], halo_recv.at[k, 2], north),
            remote(field.at[:, 1], field.at[:, ROWS + 1], halo_send.at[k, 3], halo_recv.at[k, 3], south),
        ]

    def zero_rows(field):
        @pl.when(gy == 0)
        def _():
            field[:, 0] = jnp.zeros((COLS, EDGE, HALF), BF16)

        @pl.when(gy == ngy - 1)
        def _():
            field[:, ROWS + 1] = jnp.zeros((COLS, EDGE, HALF), BF16)

    def apply_curl(field, low, high, use, after=None):
        for col in range(COLS):
            @pl.loop(0, ROWS, unroll=4)
            def _(row):
                lower = low[link_ref[0, row]] if col == 0 else field[0, row + 1]
                upper = field[1, row + 1] if col == 0 else high[link_ref[1, row]]
                near = [field[col, row + 1], lower, upper, field[col, row], field[col, row + 2]]
                tiles = [blocks_ref[adj_ref[s, col, row]] for s in range(5)]
                image = jnp.dot(
                    jnp.concatenate(tiles, axis=1), jnp.concatenate(near, axis=0), preferred_element_type=F32
                )
                use(col, row, col * ROWS + row, image)

            if after is not None:
                after(col)

    def column(c):
        return pl.ds(c * HALF, HALF)

    def own(field):
        return lambda col: field[col, pl.ds(1, ROWS)]

    def other(field):
        return lambda col: field[pl.ds(col * ROWS, ROWS)]

    row_refs = (own(fx), own(fw), own(fp), own(fa), other(p_far), other(w_far))

    def gram(g):
        rows, columns = GROUPS[g]
        wide = len(columns) * HALF
        for col in range(COLS):
            left = jnp.concatenate([row_refs[r](col).reshape(ROWS * EDGE, HALF) for r in rows], axis=1)
            right = images[pl.ds(col * ROWS, ROWS), :, pl.ds(columns[0] * HALF, wide)].reshape(ROWS * EDGE, wide)
            product = lax.dot_general(left, right, (((0,), (0,)), ((), ())), preferred_element_type=F32)
            for r in range(len(rows)):
                for c in range(len(columns)):
                    tile = pl.ds((STARTS[g] + r * len(columns) + c) * HALF, HALF)
                    value = product[r * HALF : (r + 1) * HALF, c * HALF : (c + 1) * HALF]
                    part[tile] = value if col == 0 else part[tile] + value

    def reducer(g):
        base, count = STARTS[g] * HALF, SIZES[g]
        half_rows, piece_rows = count * 64, count * 8
        half_base, piece_base = STARTS[g] * 64, STARTS[g] * 8

        def rows_of(offset, size):
            return pl.ds(pl.multiple_of(offset, 16), size)

        mine = rows_of(base + core * half_rows, half_rows)
        theirs = rows_of(base + (1 - core) * half_rows, half_rows)
        my_half = pl.ds(half_base, half_rows)
        my_piece = pl.ds(piece_base, piece_rows)
        piece_total = rows_of(base + core * half_rows + z_id * piece_rows, piece_rows)

        def core_copy():
            return remote(part.at[theirs], core_buf.at[my_half], core_send.at[g], core_recv.at[g], pair)

        def z_copy(step):
            z_to, device = z_peer(step)
            return remote(
                z_out.at[rows_of(half_base + z_to * piece_rows, piece_rows)], z_buf.at[z_id, my_piece],
                z_send.at[g, step - 1], z_recv.at[g, step - 1], device,
            )

        def b_copy(step):
            return remote(
                b_src.at[my_piece], b_buf.at[b_id, my_piece],
                b_send.at[g, step - 1], b_recv.at[g, step - 1], b_peer(step),
            )

        def back_copy(step):
            return remote(
                total_buf.at[piece_total], total_buf.at[piece_total],
                back_send.at[g, step - 1], back_recv.at[g, step - 1], z_peer(step)[1],
            )

        def pair_copy():
            return remote(total_buf.at[mine], total_buf.at[mine], pair_send.at[g], pair_recv.at[g], pair)

        def each(copy, act):
            @pl.loop(1, NZ)
            def _(step):
                act(copy(step))

        def start_core():
            core_copy().start()

        def start_z():
            core_copy().wait()
            z_out[my_half] = (part[mine] + core_buf[my_half]).astype(BF16)
            each(z_copy, lambda c: c.start())

        def start_b():
            total = part[piece_total] + core_buf[rows_of(half_base + z_id * piece_rows, piece_rows)]
            each(z_copy, lambda c: c.wait())
            for step in range(1, NZ):
                total = total + z_buf[lax.rem(z_id + step, NZ), my_piece].astype(F32)
            b_src[my_piece] = total.astype(BF16)
            b_buf[b_id, my_piece] = total.astype(BF16)
            each(b_copy, lambda c: c.start())

        def start_back():
            each(b_copy, lambda c: c.wait())
            total = b_buf[0, my_piece].astype(F32)
            for slot in range(1, NB):
                total = total + b_buf[slot, my_piece].astype(F32)
            total_buf[piece_total] = total.astype(BF16)
            each(back_copy, lambda c: c.start())

        def start_pair():
            each(back_copy, lambda c: c.wait())
            pair_copy().start()

        def finish():
            pair_copy().wait()

        return start_core, start_z, start_b, start_back, start_pair, finish

    first, second, third = reducer(0), reducer(1), reducer(2)

    def cross(k, field, target):
        return [remote(field.at[c, pl.ds(1, ROWS)], target(c), far_send.at[k, c], far_recv.at[k, c], far) for c in range(COLS)]

    x_halo, p_halo, w_halo, a_halo = halo(0, fx, xlo, xhi), halo(1, fp, plo, phi), halo(2, fw, wlo, whi), halo(3, fa, alo, ahi)
    x_cross = cross(0, fx, lambda c: fa.at[c, pl.ds(1, ROWS)])
    p_cross = cross(1, fp, lambda c: p_far.at[pl.ds(c * ROWS, ROWS)])
    start(x_halo)
    start(x_cross)
    ritz_copy.start()

    for col in range(COLS):
        @pl.loop(0, ROWS, unroll=2)
        def _(row):
            patch = col * ROWS + row
            weight = eps[patch]
            images[patch, :, column(MX)] = (weight * fx[col, row + 1].astype(F32)).astype(BF16)
            images[patch, :, column(MP)] = (weight * fp[col, row + 1].astype(F32)).astype(BF16)

    wait(x_halo)
    start(p_halo)
    zero_rows(fx)

    def use_x(col, row, patch, image):
        weight = eps[patch]
        resid = (image - weight * fx[col, row + 1].astype(F32) * ritz_ref[...]).astype(BF16)
        fw[col, row + 1] = resid
        images[patch, :, column(KX)] = image.astype(BF16)
        images[patch, :, column(MW)] = (weight * resid.astype(F32)).astype(BF16)

    apply_curl(fx, xlo, xhi, use_x, lambda col: w_halo[col].start())
    start(w_halo[2:])
    gram(0)
    first[0]()
    wait(x_cross)
    start(a_halo)
    start(p_cross)
    first[1]()
    wait(p_halo)
    zero_rows(fp)

    def use_p(col, row, patch, image):
        images[patch, :, column(KP)] = image.astype(BF16)

    apply_curl(fp, plo, phi, use_p)
    wait(w_halo)
    zero_rows(fw)
    first[2]()

    def use_w(col, row, patch, image):
        images[patch, :, column(KW)] = image.astype(BF16)

    apply_curl(fw, wlo, whi, use_w)
    first[3]()
    gram(1)
    second[0]()
    first[4]()
    wait(a_halo)
    ritz_copy.wait()
    zero_rows(fa)
    second[1]()

    def use_a(col, row, patch, image):
        w_far[patch] = (image - eps[patch] * fa[col, row + 1].astype(F32) * ritz_in[pl.ds(0, 1)]).astype(BF16)

    apply_curl(fa, alo, ahi, use_a)
    first[5]()

    row_ids = lax.broadcasted_iota(jnp.int32, (HALF, HALF), 0)
    col_ids = lax.broadcasted_iota(jnp.int32, (HALF, HALF), 1)
    diagonal = row_ids == col_ids
    norms = jnp.where(diagonal, total_buf[pl.ds(NORM_TILE * HALF, HALF)].astype(F32), 0.0)
    scale_row = lax.rsqrt(jnp.sum(norms, axis=0, keepdims=True) / edges_total + 1e-06)
    scale_col = lax.rsqrt(jnp.sum(norms, axis=1, keepdims=True) / edges_total + 1e-06)
    scale_out[...] = jnp.broadcast_to(scale_row, (8, HALF))
    scale_copy = remote(scale_out, scale_in, scale_send, scale_recv, far)
    scale_copy.start()
    second[2]()
    wait(p_cross)
    gram(2)
    third[0]()
    second[3]()
    scale_copy.wait()
    far_row = jnp.broadcast_to(scale_in[pl.ds(0, 1)], (HALF, HALF))
    far_col = jnp.sum(jnp.where(diagonal, far_row, 0.0), axis=1, keepdims=True)

    cols = pl.ds(pl.multiple_of(ma * HALF, HALF), HALF)
    for k, (block, side) in enumerate(ROW_OF):
        half = ma if side == 0 else 1 - ma
        tile = coef_ref[block, pl.ds(pl.multiple_of(half * HALF, HALF), HALF), cols]
        if block == 1:
            tile = (tile.astype(F32) * (scale_col if side == 0 else far_col)).astype(BF16)
        coef_own[pl.ds(k * HALF, HALF)] = tile

    third[1]()
    second[4]()
    for col in range(COLS):
        @pl.loop(0, ROWS, step=4)
        def _(row):
            panel = jnp.concatenate(
                [f[col, pl.ds(row + 1, 4)] for f in (fx, fw, fp, fa)]
                + [f[pl.ds(col * ROWS + row, 4)] for f in (p_far, w_far)],
                axis=2,
            ).reshape(4 * EDGE, 6 * HALF)
            rotated = jnp.dot(panel, coef_own[...], preferred_element_type=F32)
            next_ref[col, pl.ds(row, 4)] = rotated.astype(BF16).reshape(4, EDGE, HALF)

    third[2]()
    inverse = 1.0 / edges_total

    def rescale(g):
        rows, columns = GROUPS[g]
        for r, row in enumerate(rows):
            block, side = ROW_OF[row]
            factor = inverse
            if block == 1:
                factor = (scale_col if side == 0 else far_col) * inverse
            half = ma if side == 0 else 1 - ma
            place = pl.ds(pl.multiple_of(half * HALF, HALF), HALF)
            for c, col in enumerate(columns):
                tile = STARTS[g] + r * len(columns) + c
                value = total_buf[pl.ds(tile * HALF, HALF)].astype(F32) * factor
                if col in (KW, MW):
                    value = value * scale_row
                out = gk_ref if col in (KX, KW, KP) else gm_ref
                out[block, {KX: 0, MX: 0, KW: 1, MW: 1, KP: 2, MP: 2}[col], place] = value

    rescale(0)
    second[5]()
    rescale(1)
    third[3]()
    third[4]()
    third[5]()
    rescale(2)


def on_device(x_modes, p_dirs, permittivity, ritz_values, blocks, adj_types, x_link, coeffs):
    edges_total = PATCHES * EDGE * lax.axis_size("gx") * lax.axis_size("gy")
    field = pltpu.VMEM((COLS, ROWS + 2, EDGE, HALF), BF16)
    face = pltpu.VMEM((ROWS, EDGE, HALF), BF16)
    whole = pltpu.VMEM((PATCHES, EDGE, HALF), BF16)
    dma = pltpu.SemaphoreType.DMA
    vmem = pl.BlockSpec(memory_space=pltpu.VMEM)
    smem = pl.BlockSpec(memory_space=pltpu.SMEM)
    hbm = pl.BlockSpec(memory_space=pl.ANY)
    lines = TILES * HALF
    x_next, gram_k, gram_m = pl.pallas_call(
        functools.partial(step_kernel, float(edges_total)),
        out_shape=[
            jax.ShapeDtypeStruct((COLS, ROWS, EDGE, HALF), BF16),
            jax.ShapeDtypeStruct((3, 3, 2 * HALF, HALF), F32),
            jax.ShapeDtypeStruct((3, 3, 2 * HALF, HALF), F32),
        ],
        in_specs=[hbm, hbm, vmem, vmem, vmem, smem, smem, vmem],
        out_specs=[vmem, vmem, vmem],
        scratch_shapes=[
            field, field, field, field, face, face, face, face, face, face, face, face, whole, whole,
            pltpu.VMEM((PATCHES, EDGE, HALF), F32),
            pltpu.VMEM((PATCHES, EDGE, 6 * HALF), BF16),
            pltpu.VMEM((lines, HALF), F32),
            pltpu.VMEM((lines // 2, HALF), F32),
            pltpu.VMEM((lines // 2, HALF), BF16),
            pltpu.VMEM((NZ, lines // 16, HALF), BF16),
            pltpu.VMEM((lines // 16, HALF), BF16),
            pltpu.VMEM((NB, lines // 16, HALF), BF16),
            pltpu.VMEM((lines, HALF), BF16),
            pltpu.VMEM((6 * HALF, HALF), BF16),
            pltpu.VMEM((8, HALF), F32),
            pltpu.VMEM((8, HALF), F32),
            pltpu.VMEM((8, HALF), F32),
            pltpu.VMEM((8, HALF), F32),
            dma((2,)), dma((4, 4)), dma((4, 4)), dma((2, 2)), dma((2, 2)),
            dma((3,)), dma((3,)), dma((3, 7)), dma((3, 7)), dma((3, 7)), dma((3, 7)),
            dma((3, 7)), dma((3, 7)), dma((3,)), dma((3,)), dma, dma, dma, dma,
        ],
        compiler_params=pltpu.CompilerParams(
            collective_id=0, has_side_effects=True, vmem_limit_bytes=56 * 1024 * 1024
        ),
        name="lobpcg_step",
    )(
        x_modes, p_dirs, permittivity.transpose(1, 0, 2), ritz_values.reshape(1, HALF), blocks,
        adj_types, x_link.reshape(2, ROWS), coeffs,
    )
    return x_next, gram_k.transpose(0, 2, 1, 3), gram_m.transpose(0, 2, 1, 3)


def solution(mesh):
    placed = (
        P("gx", "gy", None, "ma"),
        P("gx", "gy", None, "ma"),
        P("gx", "gy", None),
        P("ma"),
        P(),
        P(None, "gx", "gy"),
        P(None, "gx", "gy"),
        P(),
    )
    return jax.shard_map(
        on_device,
        mesh=mesh,
        in_specs=placed,
        out_specs=(P("gx", "gy", None, "ma"), P(None, None, None, "ma"), P(None, None, None, "ma")),
        check_vma=False,
    )
```

profile of v0, /device:TPU:1, one launch (start us, length us, event | category | flops | bytes accessed | tf_op | source)
XLA Modules:
  0.0 108.4 jit_solution(8313624608434164739)
XLA Ops:
  0.6 102.8 %lobpcg_step.1 = (bf16[2,12,128,128]{3,2,1,0:T(8,128)(2,1)}, f32[3,3,256,128]{3,2,1,0:T(8,128)}, f32[3,3,256,128]{3,2,1,0:T(8,128)}) custom-call(bf16[2,12,128,128]{3,2,1,0:T(8,128)(2,1)} %x_hbm.1, bf16[2,12,128,128]{3,2,1,0:T(8,128)(2,1)} %p_hbm.1, f32[12,2,128]{2,1,0:T(2,128)} %bitcast.7, f32[1,128]{1,0:T(1,128)} %bitcast.9, ...), custom_call_target="tpu_custom_call" | custom-call | tf_op jit(solution)/shard_map/lobpcg_step/pallas_call | solution.py:378
  103.5 0.0 copy-start.1
  103.5 2.2 %copy.14 = bf16[2,12,128,128]{3,2,1,0:T(8,128)(2,1)} copy(bf16[2,12,128,128]{3,2,1,0:T(8,128)(2,1)} %get-tuple-element.12) | data formatting | bytes 1572864
  105.7 0.0 copy-done.1
  105.7 0.0 copy-start
  105.7 1.0 copy.15
  106.7 0.7 copy-done
  107.4 1.0 copy.16
Async XLA Ops:
  103.5 2.2 %copy-start.1 = (f32[3,3,256,128]{3,2,1,0:T(8,128)S(1)}, f32[3,3,256,128]{3,2,1,0:T(8,128)}, u32[]{:S(2)}) copy-start(f32[3,3,256,128]{3,2,1,0:T(8,128)} %get-tuple-element.7) | copy-start | bytes 3538948
  105.7 1.7 %copy-start = (f32[3,3,256,128]{3,2,1,0:T(8,128)S(1)}, f32[3,3,256,128]{3,2,1,0:T(8,128)}, u32[]{:S(2)}) copy-start(f32[3,3,256,128]{3,2,1,0:T(8,128)} %get-tuple-element.8) | copy-start | bytes 3538948
where the time goes:
time: 109 us; the launch traced here: 108 us
  Pallas kernels  103 us (94%)
  local copies, waits for them, and re-layouts  4.9 us (4%)
    pallas_call x1, Pallas kernels, on_device(): pl.pallas_call(functools.partial(step_kernel, float(edges_total)), out_sh...  103 us
    unnamed x7, local copies, waits for them, and re-layouts  4.9 us

commit v1 on v0

--- a/solution.py
+++ b/solution.py
@@ -18,11 +18,12 @@
 NB = 8
 KX, MX, MW, MP, KW, KP = range(6)
 ROW_OF = ((0, 0), (1, 0), (2, 0), (0, 1), (2, 1), (1, 1))
-GROUPS = (((0, 1, 2), (KX, MX, MW, MP)), ((0, 1, 2), (KW, KP)), ((3, 4, 5), (KX, MX, MW, MP, KW, KP)))
+ALL = (KX, MX, MW, MP, KW, KP)
+GROUPS = (((0, 1, 2), ALL), ((3, 4, 5), ALL))
 SIZES = tuple(len(r) * len(c) for r, c in GROUPS)
 STARTS = tuple(sum(SIZES[:g]) for g in range(len(SIZES)))
 TILES = sum(SIZES)
-NORM_TILE = 1 * 4 + MW
+NORM_TILE = len(ALL) + MW
 
 
 def step_kernel(
@@ -30,9 +31,9 @@
     x_hbm, p_hbm, perm_ref, ritz_ref, blocks_ref, adj_ref, link_ref, coef_ref,
     next_ref, gk_ref, gm_ref,
     fx, fp, fw, fa, xlo, xhi, plo, phi, wlo, whi, alo, ahi, p_far, w_far,
-    eps, images, part, core_buf, z_out, z_buf, b_src, b_buf, total_buf, coef_own, scale_out, scale_in, ritz_out, ritz_in,
+    eps, images, part, core_buf, b_out, b_buf, z_src, z_buf, total_buf, coef_own, scale_out, scale_in, ritz_out, ritz_in,
     load_sem, halo_send, halo_recv, far_send, far_recv,
-    core_send, core_recv, z_send, z_recv, b_send, b_recv,
+    core_send, core_recv, b_send, b_recv, z_send, z_recv,
     back_send, back_recv, pair_send, pair_recv, scale_send, scale_recv, ritz_send, ritz_recv,
 ):
     gx, gy, ma = (lax.axis_index(a) for a in ("gx", "gy", "ma"))
@@ -45,12 +46,11 @@
     far, pair = {"ma": 1 - ma}, {"gy": gy + 1 - 2 * core}
 
     def z_peer(step):
-        z_to = lax.rem(z_id + step, NZ)
-        return z_to, {"gx": y_id * NZ + z_to}
+        return {"gx": y_id * NZ + lax.rem(z_id + step, NZ)}
 
     def b_peer(step):
         b_to = lax.rem(b_id + step, NB)
-        return {"gx": (b_to // 2) * NZ + z_id, "gy": lax.rem(b_to, 2) * 2 + core}
+        return b_to, {"gx": (b_to // 2) * NZ + z_id, "gy": lax.rem(b_to, 2) * 2 + core}
 
     def remote(src, dst, send, recv, device):
         return pltpu.make_async_remote_copy(
@@ -77,21 +77,16 @@
 
     @pl.loop(1, NZ)
     def _(step):
-        pl.semaphore_signal(barrier, inc=1, device_id=z_peer(step)[1], device_id_type=MESH)
+        pl.semaphore_signal(barrier, inc=1, device_id=z_peer(step), device_id_type=MESH)
 
     @pl.loop(1, NB)
     def _(step):
-        pl.semaphore_signal(barrier, inc=1, device_id=b_peer(step), device_id_type=MESH)
-
-    for col in range(COLS):
-        @pl.loop(0, ROWS, unroll=4)
-        def _(row):
-            eps[col * ROWS + row] = jnp.broadcast_to(perm_ref[row, pl.ds(col, 1)], (EDGE, EDGE)).T
+        pl.semaphore_signal(barrier, inc=1, device_id=b_peer(step)[1], device_id_type=MESH)
 
     ritz_out[...] = jnp.broadcast_to(ritz_ref[...], (8, HALF))
     ritz_copy = remote(ritz_out, ritz_in, ritz_send, ritz_recv, far)
+    pl.semaphore_wait(barrier, 6 + NZ - 1 + NB - 1)
     wait(loads)
-    pl.semaphore_wait(barrier, 6 + NZ - 1 + NB - 1)
 
     def halo(k, field, low, high):
         return [
@@ -137,10 +132,12 @@
 
     row_refs = (own(fx), own(fw), own(fp), own(fa), other(p_far), other(w_far))
 
-    def gram(g):
+    def gram(g, ready=None):
         rows, columns = GROUPS[g]
         wide = len(columns) * HALF
         for col in range(COLS):
+            if ready is not None:
+                ready(col)
             left = jnp.concatenate([row_refs[r](col).reshape(ROWS * EDGE, HALF) for r in rows], axis=1)
             right = images[pl.ds(col * ROWS, ROWS), :, pl.ds(columns[0] * HALF, wide)].reshape(ROWS * EDGE, wide)
             product = lax.dot_general(left, right, (((0,), (0,)), ((), ())), preferred_element_type=F32)
@@ -162,28 +159,28 @@
         theirs = rows_of(base + (1 - core) * half_rows, half_rows)
         my_half = pl.ds(half_base, half_rows)
         my_piece = pl.ds(piece_base, piece_rows)
-        piece_total = rows_of(base + core * half_rows + z_id * piece_rows, piece_rows)
+        piece_total = rows_of(base + core * half_rows + b_id * piece_rows, piece_rows)
 
         def core_copy():
             return remote(part.at[theirs], core_buf.at[my_half], core_send.at[g], core_recv.at[g], pair)
 
+        def b_copy(step):
+            b_to, device = b_peer(step)
+            return remote(
+                b_out.at[rows_of(half_base + b_to * piece_rows, piece_rows)], b_buf.at[b_id, my_piece],
+                b_send.at[g, step - 1], b_recv.at[g, step - 1], device,
+            )
+
         def z_copy(step):
-            z_to, device = z_peer(step)
             return remote(
-                z_out.at[rows_of(half_base + z_to * piece_rows, piece_rows)], z_buf.at[z_id, my_piece],
-                z_send.at[g, step - 1], z_recv.at[g, step - 1], device,
-            )
-
-        def b_copy(step):
-            return remote(
-                b_src.at[my_piece], b_buf.at[b_id, my_piece],
-                b_send.at[g, step - 1], b_recv.at[g, step - 1], b_peer(step),
+                z_src.at[my_piece], z_buf.at[z_id, my_piece],
+                z_send.at[g, step - 1], z_recv.at[g, step - 1], z_peer(step),
             )
 
         def back_copy(step):
             return remote(
                 total_buf.at[piece_total], total_buf.at[piece_total],
-                back_send.at[g, step - 1], back_recv.at[g, step - 1], z_peer(step)[1],
+                back_send.at[g, step - 1], back_recv.at[g, step - 1], b_peer(step)[1],
             )
 
         def pair_copy():
@@ -197,25 +194,25 @@
         def start_core():
             core_copy().start()
 
+        def start_b():
+            core_copy().wait()
+            b_out[my_half] = (part[mine] + core_buf[my_half]).astype(BF16)
+            each(b_copy, lambda c: c.start())
+
         def start_z():
-            core_copy().wait()
-            z_out[my_half] = (part[mine] + core_buf[my_half]).astype(BF16)
+            total = part[piece_total] + core_buf[rows_of(half_base + b_id * piece_rows, piece_rows)]
+            each(b_copy, lambda c: c.wait())
+            for step in range(1, NZ):
+                total = total + b_buf[lax.rem(b_id + step, NB), my_piece].astype(F32)
+            z_src[my_piece] = total.astype(BF16)
+            z_buf[z_id, my_piece] = total.astype(BF16)
             each(z_copy, lambda c: c.start())
 
-        def start_b():
-            total = part[piece_total] + core_buf[rows_of(half_base + z_id * piece_rows, piece_rows)]
+        def start_zack():
             each(z_copy, lambda c: c.wait())
-            for step in range(1, NZ):
-                total = total + z_buf[lax.rem(z_id + step, NZ), my_piece].astype(F32)
-            b_src[my_piece] = total.astype(BF16)
-            b_buf[b_id, my_piece] = total.astype(BF16)
-            each(b_copy, lambda c: c.start())
-
-        def start_back():
-            each(b_copy, lambda c: c.wait())
-            total = b_buf[0, my_piece].astype(F32)
+            total = z_buf[0, my_piece].astype(F32)
             for slot in range(1, NB):
-                total = total + b_buf[slot, my_piece].astype(F32)
+                total = total + z_buf[slot, my_piece].astype(F32)
             total_buf[piece_total] = total.astype(BF16)
             each(back_copy, lambda c: c.start())
 
@@ -226,9 +223,9 @@
         def finish():
             pair_copy().wait()
 
-        return start_core, start_z, start_b, start_back, start_pair, finish
-
-    first, second, third = reducer(0), reducer(1), reducer(2)
+        return start_core, start_b, start_z, start_zack, start_pair, finish
+
+    near, away = reducer(0), reducer(1)
 
     def cross(k, field, target):
         return [remote(field.at[c, pl.ds(1, ROWS)], target(c), far_send.at[k, c], far_recv.at[k, c], far) for c in range(COLS)]
@@ -241,10 +238,11 @@
     ritz_copy.start()
 
     for col in range(COLS):
-        @pl.loop(0, ROWS, unroll=2)
+        @pl.loop(0, ROWS, unroll=4)
         def _(row):
             patch = col * ROWS + row
-            weight = eps[patch]
+            weight = jnp.broadcast_to(perm_ref[row, pl.ds(col, 1)], (EDGE, EDGE)).T
+            eps[patch] = weight
             images[patch, :, column(MX)] = (weight * fx[col, row + 1].astype(F32)).astype(BF16)
             images[patch, :, column(MP)] = (weight * fp[col, row + 1].astype(F32)).astype(BF16)
 
@@ -261,12 +259,9 @@
 
     apply_curl(fx, xlo, xhi, use_x, lambda col: w_halo[col].start())
     start(w_halo[2:])
-    gram(0)
-    first[0]()
     wait(x_cross)
     start(a_halo)
     start(p_cross)
-    first[1]()
     wait(p_halo)
     zero_rows(fp)
 
@@ -276,26 +271,31 @@
     apply_curl(fp, plo, phi, use_p)
     wait(w_halo)
     zero_rows(fw)
-    first[2]()
 
     def use_w(col, row, patch, image):
         images[patch, :, column(KW)] = image.astype(BF16)
 
     apply_curl(fw, wlo, whi, use_w)
-    first[3]()
-    gram(1)
-    second[0]()
-    first[4]()
+    gram(0)
+    near[0]()
     wait(a_halo)
     ritz_copy.wait()
     zero_rows(fa)
-    second[1]()
 
     def use_a(col, row, patch, image):
         w_far[patch] = (image - eps[patch] * fa[col, row + 1].astype(F32) * ritz_in[pl.ds(0, 1)]).astype(BF16)
 
     apply_curl(fa, alo, ahi, use_a)
-    first[5]()
+    near[1]()
+    wait(p_cross)
+    gram(1)
+    away[0]()
+    near[2]()
+    away[1]()
+    near[3]()
+    away[2]()
+    near[4]()
+    near[5]()
 
     row_ids = lax.broadcasted_iota(jnp.int32, (HALF, HALF), 0)
     col_ids = lax.broadcasted_iota(jnp.int32, (HALF, HALF), 1)
@@ -306,11 +306,7 @@
     scale_out[...] = jnp.broadcast_to(scale_row, (8, HALF))
     scale_copy = remote(scale_out, scale_in, scale_send, scale_recv, far)
     scale_copy.start()
-    second[2]()
-    wait(p_cross)
-    gram(2)
-    third[0]()
-    second[3]()
+    away[3]()
     scale_copy.wait()
     far_row = jnp.broadcast_to(scale_in[pl.ds(0, 1)], (HALF, HALF))
     far_col = jnp.sum(jnp.where(diagonal, far_row, 0.0), axis=1, keepdims=True)
@@ -323,8 +319,6 @@
             tile = (tile.astype(F32) * (scale_col if side == 0 else far_col)).astype(BF16)
         coef_own[pl.ds(k * HALF, HALF)] = tile
 
-    third[1]()
-    second[4]()
     for col in range(COLS):
         @pl.loop(0, ROWS, step=4)
         def _(row):
@@ -336,7 +330,6 @@
             rotated = jnp.dot(panel, coef_own[...], preferred_element_type=F32)
             next_ref[col, pl.ds(row, 4)] = rotated.astype(BF16).reshape(4, EDGE, HALF)
 
-    third[2]()
     inverse = 1.0 / edges_total
 
     def rescale(g):
@@ -357,12 +350,9 @@
                 out[block, {KX: 0, MX: 0, KW: 1, MW: 1, KP: 2, MP: 2}[col], place] = value
 
     rescale(0)
-    second[5]()
+    away[4]()
+    away[5]()
     rescale(1)
-    third[3]()
-    third[4]()
-    third[5]()
-    rescale(2)
 
 
 def on_device(x_modes, p_dirs, permittivity, ritz_values, blocks, adj_types, x_link, coeffs):
@@ -378,9 +368,9 @@
     x_next, gram_k, gram_m = pl.pallas_call(
         functools.partial(step_kernel, float(edges_total)),
         out_shape=[
-            jax.ShapeDtypeStruct((COLS, ROWS, EDGE, HALF), BF16),
-            jax.ShapeDtypeStruct((3, 3, 2 * HALF, HALF), F32),
-            jax.ShapeDtypeStruct((3, 3, 2 * HALF, HALF), F32),
+            pltpu.VMEM((COLS, ROWS, EDGE, HALF), BF16),
+            pltpu.VMEM((3, 3, 2 * HALF, HALF), F32),
+            pltpu.VMEM((3, 3, 2 * HALF, HALF), F32),
         ],
         in_specs=[hbm, hbm, vmem, vmem, vmem, smem, smem, vmem],
         out_specs=[vmem, vmem, vmem],
@@ -401,8 +391,8 @@
             pltpu.VMEM((8, HALF), F32),
             pltpu.VMEM((8, HALF), F32),
             dma((2,)), dma((4, 4)), dma((4, 4)), dma((2, 2)), dma((2, 2)),
-            dma((3,)), dma((3,)), dma((3, 7)), dma((3, 7)), dma((3, 7)), dma((3, 7)),
-            dma((3, 7)), dma((3, 7)), dma((3,)), dma((3,)), dma, dma, dma, dma,
+            dma((2,)), dma((2,)), dma((2, 7)), dma((2, 7)), dma((2, 7)), dma((2, 7)),
+            dma((2, 7)), dma((2, 7)), dma((2,)), dma((2,)), dma, dma, dma, dma,
         ],
         compiler_params=pltpu.CompilerParams(
             collective_id=0, has_side_effects=True, vmem_limit_bytes=56 * 1024 * 1024

time: 109 us -> 85.2 us (0.78)
  Pallas kernels: 103 us -> 81.6 us
  local copies, waits for them, and re-layouts: 4.9 us -> 2.91 us
    pallas_call x1, Pallas kernels: 103 us -> 81.6 us  [on_device(): pl.pallas_call(functools.partial(step_kernel, float(edges_total)), out_sh...]
    unnamed x7 -> x3, local copies, waits for them, and re-layouts: 4.9 us -> 2.91 us
where the time goes in v1:
time: 85.2 us; the launch traced here: 85.1 us
  Pallas kernels  81.6 us (96%)
  local copies, waits for them, and re-layouts  2.91 us (3%)
    pallas_call x1, Pallas kernels, on_device(): pl.pallas_call(functools.partial(step_kernel, float(edges_total)), out_sh...  81.6 us
    unnamed x3, local copies, waits for them, and re-layouts  2.91 us

profile of v1, /device:TPU:1, one launch (start us, length us, event | category | flops | bytes accessed | tf_op | source)
XLA Modules:
  0.0 85.1 jit_solution(428375308174619480)
XLA Ops:
  0.6 81.6 %lobpcg_step.1 = (bf16[2,12,128,128]{3,2,1,0:T(8,128)(2,1)S(1)}, f32[3,3,256,128]{3,2,1,0:T(8,128)S(1)}, f32[3,3,256,128]{3,2,1,0:T(8,128)S(1)}) custom-call(bf16[2,12,128,128]{3,2,1,0:T(8,128)(2,1)} %x_hbm.1, bf16[2,12,128,128]{3,2,1,0:T(8,128)(2,1)} %p_hbm.1, f32[12,2,128]{2,1,0:T(2,128)} %bitcast.7, f32[1,128]{1,0:T(1,128)} %bitcast.9, ...), custom_call_target="tpu_custom_call" | custom-call | tf_op jit(solution)/shard_map/lobpcg_step/pallas_call | solution.py:368
  82.2 0.9 %copy.14 = bf16[2,12,128,128]{3,2,1,0:T(8,128)(2,1)} copy(bf16[2,12,128,128]{3,2,1,0:T(8,128)(2,1)S(1)} %get-tuple-element.9) | data formatting | bytes 1572864
  83.1 1.0 %copy.15 = f32[3,256,3,128]{3,1,2,0:T(8,128)} copy(f32[3,256,3,128]{3,1,2,0:T(8,128)S(1)} %bitcast.6) | data formatting | bytes 2359296
  84.1 1.0 %copy.16 = f32[3,256,3,128]{3,1,2,0:T(8,128)} copy(f32[3,256,3,128]{3,1,2,0:T(8,128)S(1)} %bitcast.5) | data formatting | bytes 2359296

commit v2 on v1

--- a/solution.py
+++ b/solution.py
@@ -132,19 +132,18 @@
 
     row_refs = (own(fx), own(fw), own(fp), own(fa), other(p_far), other(w_far))
 
-    def gram(g, ready=None):
+    def gram(g, begin, end, ready=lambda col: None):
         rows, columns = GROUPS[g]
-        wide = len(columns) * HALF
+        wide = (end - begin) * HALF
         for col in range(COLS):
-            if ready is not None:
-                ready(col)
+            ready(col)
             left = jnp.concatenate([row_refs[r](col).reshape(ROWS * EDGE, HALF) for r in rows], axis=1)
-            right = images[pl.ds(col * ROWS, ROWS), :, pl.ds(columns[0] * HALF, wide)].reshape(ROWS * EDGE, wide)
+            right = images[pl.ds(col * ROWS, ROWS), :, pl.ds(begin * HALF, wide)].reshape(ROWS * EDGE, wide)
             product = lax.dot_general(left, right, (((0,), (0,)), ((), ())), preferred_element_type=F32)
             for r in range(len(rows)):
-                for c in range(len(columns)):
+                for c in range(begin, end):
                     tile = pl.ds((STARTS[g] + r * len(columns) + c) * HALF, HALF)
-                    value = product[r * HALF : (r + 1) * HALF, c * HALF : (c + 1) * HALF]
+                    value = product[r * HALF : (r + 1) * HALF, (c - begin) * HALF : (c - begin + 1) * HALF]
                     part[tile] = value if col == 0 else part[tile] + value
 
     def reducer(g):
@@ -230,9 +229,25 @@
     def cross(k, field, target):
         return [remote(field.at[c, pl.ds(1, ROWS)], target(c), far_send.at[k, c], far_recv.at[k, c], far) for c in range(COLS)]
 
-    x_halo, p_halo, w_halo, a_halo = halo(0, fx, xlo, xhi), halo(1, fp, plo, phi), halo(2, fw, wlo, whi), halo(3, fa, alo, ahi)
-    x_cross = cross(0, fx, lambda c: fa.at[c, pl.ds(1, ROWS)])
+    lead = ROWS - 4
+
+    def faces(k, field, low, high, first, count):
+        rows, place = pl.ds(1 + first, count), pl.ds(first, count)
+        side = 0 if first == 0 else 4
+        return [
+            remote(field.at[0, rows], high.at[place], halo_send.at[k, side], halo_recv.at[k, side], west),
+            remote(field.at[1, rows], low.at[place], halo_send.at[k, side + 1], halo_recv.at[k, side + 1], east),
+        ]
+
+    x_lead, x_rest = faces(0, fx, xlo, xhi, 0, lead), faces(0, fx, xlo, xhi, lead, 4)
+    x_halo, p_halo, w_halo, a_halo = halo(0, fx, xlo, xhi)[2:], halo(1, fp, plo, phi), halo(2, fw, wlo, whi), halo(3, fa, alo, ahi)
+    x_cross = [
+        remote(fx.at[c, pl.ds(1 + r, n)], fa.at[c, pl.ds(1 + r, n)], far_send.at[0, k], far_recv.at[0, k], far)
+        for k, (c, r, n) in enumerate(((0, 0, ROWS), (1, 0, ROWS - 4), (1, ROWS - 4, 4)))
+    ]
     p_cross = cross(1, fp, lambda c: p_far.at[pl.ds(c * ROWS, ROWS)])
+    start(x_lead)
+    start(x_rest)
     start(x_halo)
     start(x_cross)
     ritz_copy.start()
@@ -246,8 +261,10 @@
             images[patch, :, column(MX)] = (weight * fx[col, row + 1].astype(F32)).astype(BF16)
             images[patch, :, column(MP)] = (weight * fp[col, row + 1].astype(F32)).astype(BF16)
 
+    wait(x_lead)
+    start(p_halo)
+    wait(x_rest)
     wait(x_halo)
-    start(p_halo)
     zero_rows(fx)
 
     def use_x(col, row, patch, image):
@@ -259,9 +276,12 @@
 
     apply_curl(fx, xlo, xhi, use_x, lambda col: w_halo[col].start())
     start(w_halo[2:])
-    wait(x_cross)
+    gram(0, KX, KW)
+    wait(x_cross[:2])
+    start(p_cross[:1])
+    wait(x_cross[2:])
     start(a_halo)
-    start(p_cross)
+    start(p_cross[1:])
     wait(p_halo)
     zero_rows(fp)
 
@@ -276,7 +296,7 @@
         images[patch, :, column(KW)] = image.astype(BF16)
 
     apply_curl(fw, wlo, whi, use_w)
-    gram(0)
+    gram(0, KW, KP + 1)
     near[0]()
     wait(a_halo)
     ritz_copy.wait()
@@ -287,8 +307,7 @@
 
     apply_curl(fa, alo, ahi, use_a)
     near[1]()
-    wait(p_cross)
-    gram(1)
+    gram(1, KX, KP + 1, lambda col: p_cross[col].wait())
     away[0]()
     near[2]()
     away[1]()
@@ -390,7 +409,7 @@
             pltpu.VMEM((8, HALF), F32),
             pltpu.VMEM((8, HALF), F32),
             pltpu.VMEM((8, HALF), F32),
-            dma((2,)), dma((4, 4)), dma((4, 4)), dma((2, 2)), dma((2, 2)),
+            dma((2,)), dma((4, 6)), dma((4, 6)), dma((2, 3)), dma((2, 3)),
             dma((2,)), dma((2,)), dma((2, 7)), dma((2, 7)), dma((2, 7)), dma((2, 7)),
             dma((2, 7)), dma((2, 7)), dma((2,)), dma((2,)), dma, dma, dma, dma,
         ],

time: 85.2 us -> 85 us (level)
  no operation moved by 1% of the time
where the time goes in v2:
time: 85 us; the launch traced here: 84.9 us
  Pallas kernels  81.4 us (96%)
  local copies, waits for them, and re-layouts  2.91 us (3%)
    pallas_call x1, Pallas kernels, on_device(): pl.pallas_call(functools.partial(step_kernel, float(edges_total)), out_sh...  81.4 us
    unnamed x3, local copies, waits for them, and re-layouts  2.91 us

profile of v2, /device:TPU:1, one launch (start us, length us, event | category | flops | bytes accessed | tf_op | source)
XLA Modules:
  0.0 84.9 jit_solution(8867339895884971606)
XLA Ops:
  0.6 81.4 %lobpcg_step.1 = (bf16[2,12,128,128]{3,2,1,0:T(8,128)(2,1)S(1)}, f32[3,3,256,128]{3,2,1,0:T(8,128)S(1)}, f32[3,3,256,128]{3,2,1,0:T(8,128)S(1)}) custom-call(bf16[2,12,128,128]{3,2,1,0:T(8,128)(2,1)} %x_hbm.1, bf16[2,12,128,128]{3,2,1,0:T(8,128)(2,1)} %p_hbm.1, f32[12,2,128]{2,1,0:T(2,128)} %bitcast.7, f32[1,128]{1,0:T(1,128)} %bitcast.9, ...), custom_call_target="tpu_custom_call" | custom-call | tf_op jit(solution)/shard_map/lobpcg_step/pallas_call | solution.py:387
  82.0 0.9 %copy.14 = bf16[2,12,128,128]{3,2,1,0:T(8,128)(2,1)} copy(bf16[2,12,128,128]{3,2,1,0:T(8,128)(2,1)S(1)} %get-tuple-element.9) | data formatting | bytes 1572864
  82.9 1.0 %copy.15 = f32[3,256,3,128]{3,1,2,0:T(8,128)} copy(f32[3,256,3,128]{3,1,2,0:T(8,128)S(1)} %bitcast.6) | data formatting | bytes 2359296
  83.9 1.0 %copy.16 = f32[3,256,3,128]{3,1,2,0:T(8,128)} copy(f32[3,256,3,128]{3,1,2,0:T(8,128)S(1)} %bitcast.5) | data formatting | bytes 2359296

commit v3 on v2

--- a/solution.py
+++ b/solution.py
@@ -351,7 +351,7 @@
 
     inverse = 1.0 / edges_total
 
-    def rescale(g):
+    def rescale(g, begin, end):
         rows, columns = GROUPS[g]
         for r, row in enumerate(rows):
             block, side = ROW_OF[row]
@@ -361,6 +361,8 @@
             half = ma if side == 0 else 1 - ma
             place = pl.ds(pl.multiple_of(half * HALF, HALF), HALF)
             for c, col in enumerate(columns):
+                if not begin <= r * len(columns) + c < end:
+                    continue
                 tile = STARTS[g] + r * len(columns) + c
                 value = total_buf[pl.ds(tile * HALF, HALF)].astype(F32) * factor
                 if col in (KW, MW):
@@ -368,10 +370,27 @@
                 out = gk_ref if col in (KX, KW, KP) else gm_ref
                 out[block, {KX: 0, MX: 0, KW: 1, MW: 1, KP: 2, MP: 2}[col], place] = value
 
-    rescale(0)
+    rescale(0, 0, SIZES[0])
     away[4]()
+    middle = SIZES[1] // 2
+
+    @pl.when(core == 0)
+    def _():
+        rescale(1, 0, middle)
+
+    @pl.when(core == 1)
+    def _():
+        rescale(1, middle, SIZES[1])
+
     away[5]()
-    rescale(1)
+
+    @pl.when(core == 0)
+    def _():
+        rescale(1, middle, SIZES[1])
+
+    @pl.when(core == 1)
+    def _():
+        rescale(1, 0, middle)
 
 
 def on_device(x_modes, p_dirs, permittivity, ritz_values, blocks, adj_types, x_link, coeffs):

time: 85 us -> 85 us (level)
  no operation moved by 1% of the time
where the time goes in v3:
time: 85 us; the launch traced here: 84.9 us
  Pallas kernels  81.3 us (96%)
  local copies, waits for them, and re-layouts  2.91 us (3%)
    pallas_call x1, Pallas kernels, on_device(): pl.pallas_call(functools.partial(step_kernel, float(edges_total)), out_sh...  81.3 us
    unnamed x3, local copies, waits for them, and re-layouts  2.91 us

profile of v3, /device:TPU:1, one launch (start us, length us, event | category | flops | bytes accessed | tf_op | source)
XLA Modules:
  0.0 84.9 jit_solution(8479718253783301757)
XLA Ops:
  0.6 81.3 %lobpcg_step.1 = (bf16[2,12,128,128]{3,2,1,0:T(8,128)(2,1)S(1)}, f32[3,3,256,128]{3,2,1,0:T(8,128)S(1)}, f32[3,3,256,128]{3,2,1,0:T(8,128)S(1)}) custom-call(bf16[2,12,128,128]{3,2,1,0:T(8,128)(2,1)} %x_hbm.1, bf16[2,12,128,128]{3,2,1,0:T(8,128)(2,1)} %p_hbm.1, f32[12,2,128]{2,1,0:T(2,128)} %bitcast.7, f32[1,128]{1,0:T(1,128)} %bitcast.9, ...), custom_call_target="tpu_custom_call" | custom-call | tf_op jit(solution)/shard_map/lobpcg_step/pallas_call | solution.py:406
  82.0 0.9 %copy.14 = bf16[2,12,128,128]{3,2,1,0:T(8,128)(2,1)} copy(bf16[2,12,128,128]{3,2,1,0:T(8,128)(2,1)S(1)} %get-tuple-element.9) | data formatting | bytes 1572864
  82.9 1.0 %copy.15 = f32[3,256,3,128]{3,1,2,0:T(8,128)} copy(f32[3,256,3,128]{3,1,2,0:T(8,128)S(1)} %bitcast.6) | data formatting | bytes 2359296
  83.9 1.0 %copy.16 = f32[3,256,3,128]{3,1,2,0:T(8,128)} copy(f32[3,256,3,128]{3,1,2,0:T(8,128)S(1)} %bitcast.5) | data formatting | bytes 2359296
